TPU v7x, 32 devices: a whole 2x2x4 slice. The times are simulated.
32 devices in a mesh: section: 4 (over y, x), dp: 8 (over z, core).
Axes of the slice: x: 2, y: 2, z: 4, core: 2. Of those that a mesh axis runs over, the one named last changes fastest.
Arguments:
- states_in: bfloat16 [16, 1024, 512], P('dp', None, 'section'), may hold values from -6 to 6
- memory: bfloat16 [16, 1024, 512], P('dp', None, 'section'), may hold values from -6 to 6
- cotangent: bfloat16 [16, 1024, 512], P('dp', None, 'section'), may hold values from -6 to 6
- weight_bank: bfloat16 [4, 8, 512, 512], P('section')
- gain_bank: float32 [4, 2, 512], P('section'), may hold values from 0.1 to 1.9
- segments: int32 [16, 1024], P('dp'), may hold values from 0 to 7, as said below
- pad_mask: int32 [16, 1024], P('dp'), may hold values from 0 to 1, as said below
- memory_segments: int32 [16, 1024], P('dp'), may hold values from 0 to 7, as said below
- memory_mask: int32 [16, 1024], P('dp'), may hold values from 0 to 1, as said below
- exit_depths: int32 [16, 8], P('dp'), may hold values from 1 to 2
Outputs:
- states: bfloat16 [16, 1024, 512], P('dp', None, 'section')
- halting: float32 [16, 2, 1024], P('dp', None, 'section')
- input_grad: float32 [16, 1024, 512], P('dp', None, 'section')
- memory_grad: float32 [16, 1024, 512], P('dp', None, 'section')
- bank_grad: float32 [4, 8, 512, 512], P('section')
- gain_grad: float32 [4, 2, 512], P('section')
Inputs may be any that keep to these rules, and one draw needn't show every extreme that they name: `segments`: each row holds 8 sentences numbered in order from 0, each at least two filled slots long; the padding slots after a row's filled slots carry the number 8 - 1. `pad_mask`: a row's filled slots come first, its padding after them. `memory_segments`: each row's memory holds 8 source sentences numbered in order from 0, each at least two filled slots long; padding slots after them carry the number 8 - 1. `memory_mask`: a row's filled memory slots come first, its padding after them. `exit_depths`: a sentence of depth 1 leaves after the first layer, of depth 2 after the second.
All inputs are finite; a program needn't handle non-finite values.
Results may differ from a plain program's by a relative error of at most 0.025.
Values may be sent and summed in bfloat16 or wider, within the bound.
A program may use at most 256 MiB of HBM per device.

v0:
```python
import jax
import jax.numpy as jnp
from jax import lax
from jax.sharding import PartitionSpec as P

HEADS = 8


eps = 1e-06
block_rows = 512


def shifted(value, axis, steps):
    count = lax.axis_size(axis)
    initial, last = (max(0, -steps), min(count, count - steps))
    return lax.ppermute(value, axis, [(source, source + steps) for source in range(initial, last)])


def rms_norm(state, gain):
    return state * lax.rsqrt(jnp.mean(state * state, axis=-1, keepdims=True) + eps) * gain


def smooth_gate(values):
    return jax.nn.gelu(values, approximate=True)


def row_masks(segments, pad_mask, memory_segments, memory_mask, depths):
    places = jnp.arange(segments.shape[0])
    self_allow = (
        (segments[:, None] == segments[None, :])
        & (places[None, :] <= places[:, None])
        & ((pad_mask[None, :] == 1) | (pad_mask[:, None] == 0))
    )
    cross_allow = (memory_segments[None, :] == segments[:, None]) & (memory_mask[None, :] == 1) | (
        pad_mask[:, None] == 0
    )
    table = segments[:, None] == jnp.arange(depths.shape[0])[None, :]
    token_depth = jnp.sum(jnp.where(table, depths[None, :], 0), axis=1)
    return (self_allow, cross_allow, token_depth)


def block_spans(length):
    count = max(1, length // block_rows)
    return (count, length // count)


def attend_core(query, keys, values, allowed, heads):
    length, width = query.shape
    size = width // heads
    scale = size ** (-0.5)
    key_heads = keys.reshape(-1, heads, size)
    value_heads = values.reshape(-1, heads, size)
    count, span = block_spans(length)
    pieces = []
    totals = []
    for block in range(count):
        begin = block * span
        query_heads = query[begin : begin + span].reshape(span, heads, size)
        scores = (
            jnp.einsum("qhe,khe->hqk", query_heads, key_heads, preferred_element_type=jnp.float32)
            * scale
        )
        scores = jnp.where(allowed[None, begin : begin + span], scores, -1e30)
        highest = jnp.max(scores, axis=-1, keepdims=True)
        expo = jnp.exp(scores - highest)
        summed = jnp.sum(expo, axis=-1, keepdims=True)
        probs = (expo / summed).astype(jnp.bfloat16)
        pieces.append(
            jnp.einsum(
                "hqk,khe->qhe", probs, value_heads, preferred_element_type=jnp.float32
            ).reshape(span, width)
        )
        totals.append(highest[..., 0] + jnp.log(summed[..., 0]))
    return (jnp.concatenate(pieces, axis=0).astype(jnp.bfloat16), jnp.concatenate(totals, axis=1))


def attend_core_back(query, keys, values, allowed, log_total, grad_mixed, heads):
    length, width = query.shape
    size = width // heads
    scale = size ** (-0.5)
    key_heads = keys.reshape(-1, heads, size)
    value_heads = values.reshape(-1, heads, size)
    count, span = block_spans(length)
    grad_key_sum = jnp.zeros(key_heads.shape, jnp.float32)
    grad_value_sum = jnp.zeros(value_heads.shape, jnp.float32)
    mixed_pieces = []
    query_pieces = []
    for block in range(count):
        begin = block * span
        query_heads = query[begin : begin + span].reshape(span, heads, size)
        scores = (
            jnp.einsum("qhe,khe->hqk", query_heads, key_heads, preferred_element_type=jnp.float32)
            * scale
        )
        scores = jnp.where(allowed[None, begin : begin + span], scores, -1e30)
        probs_full = jnp.exp(scores - log_total[:, begin : begin + span, None])
        probs = probs_full.astype(jnp.bfloat16)
        mixed_pieces.append(
            jnp.einsum(
                "hqk,khe->qhe", probs, value_heads, preferred_element_type=jnp.float32
            ).reshape(span, width)
        )
        grad_heads = grad_mixed[begin : begin + span].reshape(span, heads, size)
        grad_probs = jnp.einsum(
            "qhe,khe->hqk", grad_heads, value_heads, preferred_element_type=jnp.float32
        )
        grad_value_sum = grad_value_sum + jnp.einsum(
            "hqk,qhe->khe", probs, grad_heads, preferred_element_type=jnp.float32
        )
        grad_scores = (
            probs_full * (grad_probs - jnp.sum(grad_probs * probs_full, axis=-1, keepdims=True))
        ).astype(jnp.bfloat16)
        query_pieces.append(
            jnp.einsum(
                "hqk,khe->qhe", grad_scores, key_heads, preferred_element_type=jnp.float32
            ).reshape(span, width)
            * scale
        )
        grad_key_sum = (
            grad_key_sum
            + jnp.einsum(
                "hqk,qhe->khe", grad_scores, query_heads, preferred_element_type=jnp.float32
            )
            * scale
        )
    mixed = jnp.concatenate(mixed_pieces, axis=0).astype(jnp.bfloat16)
    grad_query = jnp.concatenate(query_pieces, axis=0).astype(jnp.bfloat16)
    grad_keys = grad_key_sum.reshape(-1, width).astype(jnp.bfloat16)
    grad_values = grad_value_sum.reshape(-1, width).astype(jnp.bfloat16)
    return (mixed, grad_query, grad_keys, grad_values)


def attention_forward(state, source, gain, weights, allowed, onward, heads):
    normed = rms_norm(state, gain).astype(jnp.bfloat16)
    keys_from = normed if source is None else source
    query = jnp.dot(normed, weights[0], preferred_element_type=jnp.float32).astype(jnp.bfloat16)
    keys = jnp.dot(keys_from, weights[1], preferred_element_type=jnp.float32).astype(jnp.bfloat16)
    values = jnp.dot(keys_from, weights[2], preferred_element_type=jnp.float32).astype(jnp.bfloat16)
    mixed, log_total = attend_core(query, keys, values, allowed, heads)
    branch = jnp.dot(mixed, weights[3], preferred_element_type=jnp.float32)
    return (state + onward[:, None] * branch, log_total)


def attention_backward(state, source, gain, weights, allowed, onward, log_total, grad_out, heads):
    normed_full, norm_back = jax.vjp(rms_norm, state, gain)
    normed = normed_full.astype(jnp.bfloat16)
    keys_from = normed if source is None else source
    query = jnp.dot(normed, weights[0], preferred_element_type=jnp.float32).astype(jnp.bfloat16)
    keys = jnp.dot(keys_from, weights[1], preferred_element_type=jnp.float32).astype(jnp.bfloat16)
    values = jnp.dot(keys_from, weights[2], preferred_element_type=jnp.float32).astype(jnp.bfloat16)
    grad_branch = (onward[:, None] * grad_out).astype(jnp.bfloat16)
    grad_mixed = jnp.dot(grad_branch, weights[3].T, preferred_element_type=jnp.float32).astype(
        jnp.bfloat16
    )
    mixed, grad_query, grad_keys, grad_values = attend_core_back(
        query, keys, values, allowed, log_total, grad_mixed, heads
    )
    grad_output_weight = jnp.dot(mixed.T, grad_branch, preferred_element_type=jnp.float32)
    grad_query_weight = jnp.dot(normed.T, grad_query, preferred_element_type=jnp.float32)
    grad_key_weight = jnp.dot(keys_from.T, grad_keys, preferred_element_type=jnp.float32)
    grad_value_weight = jnp.dot(keys_from.T, grad_values, preferred_element_type=jnp.float32)
    grad_normed = jnp.dot(grad_query, weights[0].T, preferred_element_type=jnp.float32)
    grad_source = jnp.dot(grad_keys, weights[1].T, preferred_element_type=jnp.float32) + jnp.dot(
        grad_values, weights[2].T, preferred_element_type=jnp.float32
    )
    if source is None:
        grad_normed = grad_normed + grad_source
    grad_state, grad_gain = norm_back(grad_normed)
    grad_weights = jnp.stack(
        [grad_query_weight, grad_key_weight, grad_value_weight, grad_output_weight]
    )
    return (grad_out + grad_state, grad_weights, grad_gain, grad_source)


def feed_forward(state, gain, weights, onward):
    normed = rms_norm(state, gain).astype(jnp.bfloat16)
    hidden = jnp.einsum("td,jde->tje", normed, weights[:4], preferred_element_type=jnp.float32)
    active = smooth_gate(hidden).astype(jnp.bfloat16)
    branch = jnp.einsum("tje,jed->td", active, weights[4:], preferred_element_type=jnp.float32)
    return state + onward[:, None] * branch


def feed_forward_backward(state, gain, weights, onward, grad_out):
    normed_full, norm_back = jax.vjp(rms_norm, state, gain)
    normed = normed_full.astype(jnp.bfloat16)
    hidden = jnp.einsum("td,jde->tje", normed, weights[:4], preferred_element_type=jnp.float32)
    active_full, gate_back = jax.vjp(smooth_gate, hidden)
    active = active_full.astype(jnp.bfloat16)
    grad_branch = (onward[:, None] * grad_out).astype(jnp.bfloat16)
    grad_down = jnp.einsum("tje,td->jed", active, grad_branch, preferred_element_type=jnp.float32)
    grad_active = jnp.einsum(
        "td,jed->tje", grad_branch, weights[4:], preferred_element_type=jnp.float32
    )
    grad_hidden = gate_back(grad_active)[0].astype(jnp.bfloat16)
    grad_up = jnp.einsum("td,tje->jde", normed, grad_hidden, preferred_element_type=jnp.float32)
    grad_normed = jnp.einsum(
        "tje,jde->td", grad_hidden, weights[:4], preferred_element_type=jnp.float32
    )
    grad_state, grad_gain = norm_back(grad_normed)
    return (grad_out + grad_state, jnp.concatenate([grad_up, grad_down], axis=0), grad_gain)


def exit_terms(after, exit_vector, valid, target, sentences):
    factor = after.shape[1] ** (-0.5)
    logits = jnp.sum(after * exit_vector, axis=-1) * factor
    scores = jax.nn.sigmoid(logits)
    weight_row = valid * (scores - target) / sentences
    return (scores, jnp.sum(weight_row[:, None] * after, axis=0) * factor)


def pair_backward(
    state,
    middle,
    memory_row,
    gains,
    weights,
    self_allow,
    cross_allow,
    onward,
    totals,
    grad_out,
    heads,
):
    grad_middle, cross_weights, cross_gain, grad_source = attention_backward(
        middle, memory_row, gains[1], weights[4:], cross_allow, onward, totals[1], grad_out, heads
    )
    grad_state, self_weights, self_gain, _ = attention_backward(
        state, None, gains[0], weights[:4], self_allow, onward, totals[0], grad_middle, heads
    )
    return (
        grad_state,
        jnp.concatenate([self_weights, cross_weights], axis=0),
        jnp.stack([self_gain, cross_gain]),
        grad_source,
    )


def local(
    states_in,
    memory,
    cotangent,
    weight_bank,
    gain_bank,
    segments,
    pad_mask,
    memory_segments,
    memory_mask,
    exit_depths,
):
    section = lax.axis_index("section")
    sections = lax.axis_size("section")
    inputs, memory_rows, grads_in = (
        lax.all_gather(states_in, "section", axis=2, tiled=True),
        lax.all_gather(memory, "section", axis=2, tiled=True),
        lax.all_gather(cotangent, "section", axis=2, tiled=True),
    )
    weights = weight_bank[0]
    gains = gain_bank[0]
    micro, length, width = inputs.shape
    slots = memory_rows.shape[1]
    sentences = exit_depths.shape[1]
    first_layer = section < 2
    even = section % 2 == 0
    last = section == sections - 1
    layer = section // 2

    def row_setup(row):
        self_allow, cross_allow, depth = row_masks(
            segments[row], pad_mask[row], memory_segments[row], memory_mask[row], exit_depths[row]
        )
        onward = jnp.where(first_layer, 1.0, (depth == 2).astype(jnp.float32))
        return (self_allow, cross_allow, depth, onward)

    def forward_tick(tick, carry):
        arrived, kept, kept_middle, kept_totals, final, halting, exit_sum = carry
        index = tick - section
        live = (index >= 0) & (index < micro)
        row = jnp.clip(index, 0, micro - 1)
        self_allow, cross_allow, depth, onward = row_setup(row)
        entry = jnp.where(section == 0, inputs[row], arrived)
        state = entry.astype(jnp.float32)

        def forward_attention_section():
            middle, first_total = attention_forward(
                state, None, gains[0], weights[:4], self_allow, onward, HEADS
            )
            after, second_total = attention_forward(
                middle, memory_rows[row], gains[1], weights[4:], cross_allow, onward, HEADS
            )
            return (
                after,
                middle,
                jnp.stack([first_total, second_total]),
                jnp.zeros((length,), jnp.float32),
                jnp.zeros((width,), jnp.float32),
            )

        def forward_dense_section():
            after = feed_forward(state, gains[0], weights, onward)
            target = jnp.where(first_layer, (depth == 1).astype(jnp.float32), 1.0)
            scores, exit_grad = exit_terms(
                after, gains[1], pad_mask[row].astype(jnp.float32), target, sentences
            )
            return (
                after,
                jnp.zeros_like(state),
                jnp.zeros((2, HEADS, length), jnp.float32),
                scores,
                exit_grad,
            )

        after, middle, totals, scores, exit_grad = lax.cond(
            even, forward_attention_section, forward_dense_section
        )
        kept = kept.at[row].set(jnp.where(live, entry, kept[row]))
        kept_middle = kept_middle.at[row].set(jnp.where(live, middle, kept_middle[row]))
        kept_totals = kept_totals.at[row].set(jnp.where(live, totals, kept_totals[row]))
        final = final.at[row].set(jnp.where(live & last, after, final[row]))
        halting = halting.at[row, layer].set(
            jnp.where(live & jnp.logical_not(even), scores, halting[row, layer])
        )
        exit_sum = exit_sum + jnp.where(live, exit_grad, 0.0)
        sent = shifted(after.astype(jnp.bfloat16), "section", 1)
        return (sent, kept, kept_middle, kept_totals, final, halting, exit_sum)

    start = (
        jnp.zeros((length, width), jnp.bfloat16),
        jnp.zeros((micro, length, width), jnp.bfloat16),
        jnp.zeros((micro, length, width), jnp.float32),
        jnp.zeros((micro, 2, HEADS, length), jnp.float32),
        jnp.zeros((micro, length, width), jnp.float32),
        jnp.zeros((micro, 2, length), jnp.float32),
        jnp.zeros((width,), jnp.float32),
    )
    _, kept, kept_middle, kept_totals, final, halting, exit_sum = lax.fori_loop(
        0, micro + sections - 1, forward_tick, start
    )

    def backward_tick(tick, carry):
        arrived, grad_bank, grad_gains, grad_states, grad_memory, total_bank, total_gains = carry
        index = tick - (sections - 1 - section)
        live = (index >= 0) & (index < micro)
        row = jnp.clip(index, 0, micro - 1)
        self_allow, cross_allow, depth, onward = row_setup(row)
        incoming = jnp.where(last, grads_in[row], arrived).astype(jnp.float32)
        state = kept[row].astype(jnp.float32)

        def backward_attention_section():
            return pair_backward(
                state,
                kept_middle[row],
                memory_rows[row],
                gains,
                weights,
                self_allow,
                cross_allow,
                onward,
                kept_totals[row],
                incoming,
                HEADS,
            )

        def backward_dense_section():
            grad_state, grad_weights, grad_gain = feed_forward_backward(
                state, gains[0], weights, onward, incoming
            )
            return (
                grad_state,
                grad_weights,
                jnp.stack([grad_gain, jnp.zeros_like(grad_gain)]),
                jnp.zeros((slots, width), jnp.float32),
            )

        grad_state, grad_weights, grad_gain_pair, grad_source = lax.cond(
            even, backward_attention_section, backward_dense_section
        )
        grad_bank = grad_bank + jnp.where(live, grad_weights, 0.0)
        grad_gains = grad_gains + jnp.where(live, grad_gain_pair, 0.0)
        grad_states = grad_states.at[row].set(
            jnp.where(live & (section == 0), grad_state, grad_states[row])
        )
        grad_memory = grad_memory.at[row].add(jnp.where(live, grad_source, 0.0))
        sent = shifted(grad_state.astype(jnp.bfloat16), "section", -1)
        return (sent, grad_bank, grad_gains, grad_states, grad_memory, total_bank, total_gains)

    bank_zeros = jnp.zeros((8, width, width), jnp.float32)
    gain_start = jnp.zeros((2, width), jnp.float32).at[1].set(exit_sum)
    back_start = (
        jnp.zeros((length, width), jnp.bfloat16),
        bank_zeros,
        gain_start,
        jnp.zeros((micro, length, width), jnp.float32),
        jnp.zeros((micro, slots, width), jnp.float32),
        bank_zeros,
        jnp.zeros((2, width), jnp.float32),
    )
    ends = lax.fori_loop(0, micro + sections - 1, backward_tick, back_start)
    summed_bank, summed_gains = lax.psum((ends[1], ends[2]), "dp")
    summed_states, halting_out, grad_inputs, grad_memory = (
        lax.psum_scatter(
            final.astype(jnp.bfloat16), "section", scatter_dimension=2, tiled=True
        ).astype(jnp.float32),
        lax.psum_scatter(
            halting.astype(jnp.bfloat16), "section", scatter_dimension=2, tiled=True
        ).astype(jnp.float32),
        lax.psum_scatter(
            ends[3].astype(jnp.bfloat16), "section", scatter_dimension=2, tiled=True
        ).astype(jnp.float32),
        lax.psum_scatter(
            ends[4].astype(jnp.bfloat16), "section", scatter_dimension=2, tiled=True
        ).astype(jnp.float32),
    )
    states_out = summed_states.astype(jnp.bfloat16)
    return (
        states_out,
        halting_out,
        grad_inputs,
        grad_memory,
        summed_bank[None],
        summed_gains[None],
    )


def solution(mesh):
    return jax.shard_map(
        local,
        mesh=mesh,
        in_specs=(
            P("dp", None, "section"),
            P("dp", None, "section"),
            P("dp", None, "section"),
            P("section", None, None, None),
            P("section", None, None),
            P("dp", None),
            P("dp", None),
            P("dp", None),
            P("dp", None),
            P("dp", None),
        ),
        out_specs=(
            P("dp", None, "section"),
            P("dp", None, "section"),
            P("dp", None, "section"),
            P("dp", None, "section"),
            P("section", None, None, None),
            P("section", None, None),
        ),
        check_vma=False,
    )
```

profile of v0, /device:TPU:0, one launch (start us, length us, event | category | flops | bytes accessed | tf_op | source)
XLA Modules:
  0.0 2543.0 jit_solution(17182288091520866962)
XLA Ops:
  12.4 35.3 %all-gather.6.cloned.1.call-done = bf16[2,1024,512]{2,1,0:T(8,128)(2,1)} async-done(((bf16[2,1024,128]{2,1,0:T(8,128)(2,1)}), bf16[2,1024,512]{2,1,0:T(8,128)(2,1)}) %all-gather.6.cloned.1.call-update) | async-done | bytes 2097168 | tf_op jit(solution)/shard_map/all_gather | solution.py:254
  47.7 37.8 %all-gather.4.cloned.1.call-done = bf16[2,1024,512]{1,2,0:T(8,128)(2,1)} async-done(((bf16[2,1024,128]{1,2,0:T(8,128)(2,1)}), bf16[2,1024,512]{1,2,0:T(8,128)(2,1)}) %all-gather.4.cloned.1.call-update) | async-done | bytes 2097168 | tf_op jit(solution)/shard_map/all_gather | solution.py:253
  91.0 610.4 %while.60 = (s32[]{:T(128)}, bf16[1024,512]{0,1:T(8,128)(2,1)S(1)}, bf16[2,1024,512]{1,2,0:T(8,128)(2,1)}, f32[2,1024,512]{2,1,0:T(8,128)}, f32[2,2,8,1024]{3,2,...) while((s32[]{:T(128)}, bf16[1024,512]{0,1:T(8,128)(2,1)S(1)}, ...), condition=%wide.region_20.21_spmd.clone, body=%wide.region_0.20_spmd.clone.sunk | while | flops 8820705280 | bytes 398836224 | solution.py:335
  99.4 82.6 %conditional.6 = (bf16[1024,512]{0,1:T(8,128)(2,1)}, f32[1024,512]{0,1:T(8,128)}, f32[2,8,1024]{2,1,0:T(8,128)S(1)}, f32[1024]{0:T(1024)S(1)}, f32[512]{0:T(512)S(1)}) conditional(s32[]{:T(128)} %convert_element_type.623, (f32[1024]{0:T(1024)S(1)}, f32[1024,512]{0,1:T(8,128)S(1)}, f32[2,512]{1,0:T(2,128)S(1)}, bf16[8,512,512]{2,1,0:T(8,128)(2,1)}, ...), branch_computations={%region_2.5_spmd, %region_6.16_spmd} | conditional | flops 8815924224 | bytes 299720960 | solution.py:312
  221.9 82.6 %conditional.6 = (bf16[1024,512]{0,1:T(8,128)(2,1)}, f32[1024,512]{0,1:T(8,128)}, f32[2,8,1024]{2,1,0:T(8,128)S(1)}, f32[1024]{0:T(1024)S(1)}, f32[512]{0:T(512)S(1)}) conditional(s32[]{:T(128)} %convert_element_type.623, (f32[1024]{0:T(1024)S(1)}, f32[1024,512]{0,1:T(8,128)S(1)}, f32[2,512]{1,0:T(2,128)S(1)}, bf16[8,512,512]{2,1,0:T(8,128)(2,1)}, ...), branch_computations={%region_2.5_spmd, %region_6.16_spmd} | conditional | flops 8815924224 | bytes 299720960 | solution.py:312
  344.3 82.7 %conditional.6 = (bf16[1024,512]{0,1:T(8,128)(2,1)}, f32[1024,512]{0,1:T(8,128)}, f32[2,8,1024]{2,1,0:T(8,128)S(1)}, f32[1024]{0:T(1024)S(1)}, f32[512]{0:T(512)S(1)}) conditional(s32[]{:T(128)} %convert_element_type.623, (f32[1024]{0:T(1024)S(1)}, f32[1024,512]{0,1:T(8,128)S(1)}, f32[2,512]{1,0:T(2,128)S(1)}, bf16[8,512,512]{2,1,0:T(8,128)(2,1)}, ...), branch_computations={%region_2.5_spmd, %region_6.16_spmd} | conditional | flops 8815924224 | bytes 299720960 | solution.py:312
  465.5 82.7 %conditional.6 = (bf16[1024,512]{0,1:T(8,128)(2,1)}, f32[1024,512]{0,1:T(8,128)}, f32[2,8,1024]{2,1,0:T(8,128)S(1)}, f32[1024]{0:T(1024)S(1)}, f32[512]{0:T(512)S(1)}) conditional(s32[]{:T(128)} %convert_element_type.623, (f32[1024]{0:T(1024)S(1)}, f32[1024,512]{0,1:T(8,128)S(1)}, f32[2,512]{1,0:T(2,128)S(1)}, bf16[8,512,512]{2,1,0:T(8,128)(2,1)}, ...), branch_computations={%region_2.5_spmd, %region_6.16_spmd} | conditional | flops 8815924224 | bytes 299720960 | solution.py:312
  586.4 82.6 %conditional.6 = (bf16[1024,512]{0,1:T(8,128)(2,1)}, f32[1024,512]{0,1:T(8,128)}, f32[2,8,1024]{2,1,0:T(8,128)S(1)}, f32[1024]{0:T(1024)S(1)}, f32[512]{0:T(512)S(1)}) conditional(s32[]{:T(128)} %convert_element_type.623, (f32[1024]{0:T(1024)S(1)}, f32[1024,512]{0,1:T(8,128)S(1)}, f32[2,512]{1,0:T(2,128)S(1)}, bf16[8,512,512]{2,1,0:T(8,128)(2,1)}, ...), branch_computations={%region_2.5_spmd, %region_6.16_spmd} | conditional | flops 8815924224 | bytes 299720960 | solution.py:312
  714.9 1554.8 %while.61 = (s32[]{:T(128)}, bf16[1024,512]{1,0:T(8,128)(2,1)}, f32[8,512,512]{2,1,0:T(8,128)}, f32[2,512]{1,0:T(2,128)}, bf16[2,1024,512]{2,1,0:T(8,128)(2,1)},...) while((s32[]{:T(128)}, bf16[1024,512]{1,0:T(8,128)(2,1)}, ...), condition=%wide.region_41.42_spmd.clone, body=%wide.region_23.41_spmd.clone.sunk | while | flops 24933066752 | bytes 1102132992 | solution.py:397
  729.9 263.0 %conditional.7 = (f32[8,512,512]{2,1,0:T(8,128)}, f32[2,512]{1,0:T(2,128)}, f32[1024,512]{1,0:T(8,128)}, f32[1024,512]{1,0:T(8,128)}, f32[1024,512]{1,0:T(8,128)...) conditional(s32[]{:T(128)} %convert_element_type.626, (f32[1024]{0:T(1024)S(1)}, f32[1024,512]{1,0:T(8,128)}, ...), branch_computations={%region_25.28_spmd, %region_29.39_spmd} | conditional | flops 24919930880 | bytes 1028562048 | solution.py:374
  799.1 14.7 multiply_reduce_fusion.10
  813.9 11.8 multiply_convert_fusion.11
  912.0 14.7 multiply_reduce_fusion.8
  1010.5 15.8 collective-permute-done.1
  1042.1 262.5 %conditional.7 = (f32[8,512,512]{2,1,0:T(8,128)}, f32[2,512]{1,0:T(2,128)}, f32[1024,512]{1,0:T(8,128)}, f32[1024,512]{1,0:T(8,128)}, f32[1024,512]{1,0:T(8,128)...) conditional(s32[]{:T(128)} %convert_element_type.626, (f32[1024]{0:T(1024)S(1)}, f32[1024,512]{1,0:T(8,128)}, ...), branch_computations={%region_25.28_spmd, %region_29.39_spmd} | conditional | flops 24919930880 | bytes 1028562048 | solution.py:374
  1110.9 14.7 multiply_reduce_fusion.10
  1125.6 11.8 multiply_convert_fusion.11
  1223.7 14.7 multiply_reduce_fusion.8
  1353.0 262.5 %conditional.7 = (f32[8,512,512]{2,1,0:T(8,128)}, f32[2,512]{1,0:T(2,128)}, f32[1024,512]{1,0:T(8,128)}, f32[1024,512]{1,0:T(8,128)}, f32[1024,512]{1,0:T(8,128)...) conditional(s32[]{:T(128)} %convert_element_type.626, (f32[1024]{0:T(1024)S(1)}, f32[1024,512]{1,0:T(8,128)}, ...), branch_computations={%region_25.28_spmd, %region_29.39_spmd} | conditional | flops 24919930880 | bytes 1028562048 | solution.py:374
  1421.8 14.7 multiply_reduce_fusion.10
  1534.6 14.7 multiply_reduce_fusion.8
  1663.0 262.5 %conditional.7 = (f32[8,512,512]{2,1,0:T(8,128)}, f32[2,512]{1,0:T(2,128)}, f32[1024,512]{1,0:T(8,128)}, f32[1024,512]{1,0:T(8,128)}, f32[1024,512]{1,0:T(8,128)...) conditional(s32[]{:T(128)} %convert_element_type.626, (f32[1024]{0:T(1024)S(1)}, f32[1024,512]{1,0:T(8,128)}, ...), branch_computations={%region_25.28_spmd, %region_29.39_spmd} | conditional | flops 24919930880 | bytes 1028562048 | solution.py:374
  1731.7 14.7 multiply_reduce_fusion.10
  1746.5 11.8 multiply_convert_fusion.11
  1844.6 14.7 multiply_reduce_fusion.8
  1972.0 262.5 %conditional.7 = (f32[8,512,512]{2,1,0:T(8,128)}, f32[2,512]{1,0:T(2,128)}, f32[1024,512]{1,0:T(8,128)}, f32[1024,512]{1,0:T(8,128)}, f32[1024,512]{1,0:T(8,128)...) conditional(s32[]{:T(128)} %convert_element_type.626, (f32[1024]{0:T(1024)S(1)}, f32[1024,512]{1,0:T(8,128)}, ...), branch_computations={%region_25.28_spmd, %region_29.39_spmd} | conditional | flops 24919930880 | bytes 1028562048 | solution.py:374
  2040.8 14.7 multiply_reduce_fusion.10
  2055.5 11.8 multiply_convert_fusion.11
  2153.6 14.7 multiply_reduce_fusion.8
  2287.5 14.2 psum.15
  2314.2 35.5 %reduce-scatter.19.cloned.1.call-done = bf16[128,2048]{1,0:T(8,128)(2,1)} async-done(((bf16[512,2048]{1,0:T(8,128)(2,1)}), bf16[128,2048]{1,0:T(8,128)(2,1)}) %reduce-scatter.19.cloned.1.call-update) | async-done | bytes 524304
  2352.6 175.5 %all-reduce.4.cloned.1.call-done = f32[1,8,512,512]{3,2,1,0:T(8,128)} async-done(((f32[1,8,512,512]{3,2,1,0:T(8,128)}), f32[1,8,512,512]{3,2,1,0:T(8,128)}) %all-reduce.4.cloned.1.call-update) | async-done | bytes 8388624 | tf_op jit(solution)/shard_map/psum | solution.py:398
  (1807 shorter events, 1951.0 us)
Async XLA Ops:
  7.2 40.6 %all-gather.6.cloned.1.call-start = ((), (), s32[]{:S(2)}) async-start(), calls=%async_computation.5 | async-start | bytes 2621440 | tf_op jit(solution)/shard_map/all_gather | solution.py:254
  7.9 77.6 %all-gather.4.cloned.1.call-start = ((), (), s32[]{:S(2)}) async-start(), calls=%async_computation.4 | async-start | bytes 2621440 | tf_op jit(solution)/shard_map/all_gather | solution.py:253
  10.0 701.3 %all-gather.8.cloned.1.call-start = ((), (), s32[]{:S(2)}) async-start(), calls=%async_computation.6 | async-start | bytes 2621440 | tf_op jit(solution)/shard_map/all_gather | solution.py:255
  10.8 2291.0 %reduce-scatter.15.cloned.1.call-start = ((), (), s32[]{:S(2)}) async-start(), calls=%async_computation.9 | async-start | bytes 327680
  11.0 80.0 %copy-start.41 = (bf16[2,1024,512]{2,1,0:T(8,128)(2,1)}, bf16[2,1024,512]{2,1,0:T(8,128)(2,1)S(1)}, u32[]{:S(2)}) copy-start(bf16[2,1024,512]{2,1,0:T(8,128)(2,1)S(1)} %fusion.256) | copy-start | bytes 6291460
  12.4 78.6 %copy-start.61 = (f32[1,2,512]{2,1,0:T(2,128)S(1)}, f32[1,2,512]{2,1,0:T(2,128)}, u32[]{:S(2)}) copy-start(f32[1,2,512]{2,1,0:T(2,128)} %param.38) | copy-start | bytes 12292
  12.4 78.6 %copy-start.68 = (s32[2,1024]{1,0:T(2,128)S(1)}, s32[2,1024]{1,0:T(2,128)}, u32[]{:S(2)}) copy-start(s32[2,1024]{1,0:T(2,128)} %param.40) | copy-start | bytes 24580
  99.4 85.0 %copy-start.59 = (f32[2,2,8,1024]{3,2,1,0:T(8,128)S(1)}, f32[2,2,8,1024]{3,2,1,0:T(8,128)}, u32[]{:S(2)}) copy-start(f32[2,2,8,1024]{3,2,1,0:T(8,128)} %get-tuple-element.2605) | copy-start | bytes 393220 | tf_op jit(solution)/shard_map/while
  182.1 30.0 %collective-permute-start = (bf16[1024,512]{0,1:T(8,128)(2,1)}, bf16[1024,512]{0,1:T(8,128)(2,1)}, u32[]{:S(2)}, u32[]{:S(2)}) collective-permute-start(bf16[1024,512]{0,1:T(8,128)(2,1)} %get-tuple-element.2507), channel_id=1, source_target_pairs={{0,8},{8,16},{16,24},{1,9},{9,17},{17,25},{2,10},{10,18},{18,26},{... | collective-permute-start | bytes 3145736 | tf_op jit(solution)/shard_map/while/body/eval_jaxpr/ppermute | solution.py:16
  221.9 84.9 %copy-start.59 = (f32[2,2,8,1024]{3,2,1,0:T(8,128)S(1)}, f32[2,2,8,1024]{3,2,1,0:T(8,128)}, u32[]{:S(2)}) copy-start(f32[2,2,8,1024]{3,2,1,0:T(8,128)} %get-tuple-element.2605) | copy-start | bytes 393220 | tf_op jit(solution)/shard_map/while
  304.5 29.9 %collective-permute-start = (bf16[1024,512]{0,1:T(8,128)(2,1)}, bf16[1024,512]{0,1:T(8,128)(2,1)}, u32[]{:S(2)}, u32[]{:S(2)}) collective-permute-start(bf16[1024,512]{0,1:T(8,128)(2,1)} %get-tuple-element.2507), channel_id=1, source_target_pairs={{0,8},{8,16},{16,24},{1,9},{9,17},{17,25},{2,10},{10,18},{18,26},{... | collective-permute-start | bytes 3145736 | tf_op jit(solution)/shard_map/while/body/eval_jaxpr/ppermute | solution.py:16
  344.3 85.0 %copy-start.59 = (f32[2,2,8,1024]{3,2,1,0:T(8,128)S(1)}, f32[2,2,8,1024]{3,2,1,0:T(8,128)}, u32[]{:S(2)}) copy-start(f32[2,2,8,1024]{3,2,1,0:T(8,128)} %get-tuple-element.2605) | copy-start | bytes 393220 | tf_op jit(solution)/shard_map/while
  427.0 28.3 %collective-permute-start = (bf16[1024,512]{0,1:T(8,128)(2,1)}, bf16[1024,512]{0,1:T(8,128)(2,1)}, u32[]{:S(2)}, u32[]{:S(2)}) collective-permute-start(bf16[1024,512]{0,1:T(8,128)(2,1)} %get-tuple-element.2507), channel_id=1, source_target_pairs={{0,8},{8,16},{16,24},{1,9},{9,17},{17,25},{2,10},{10,18},{18,26},{... | collective-permute-start | bytes 3145736 | tf_op jit(solution)/shard_map/while/body/eval_jaxpr/ppermute | solution.py:16
  465.5 85.0 %copy-start.59 = (f32[2,2,8,1024]{3,2,1,0:T(8,128)S(1)}, f32[2,2,8,1024]{3,2,1,0:T(8,128)}, u32[]{:S(2)}) copy-start(f32[2,2,8,1024]{3,2,1,0:T(8,128)} %get-tuple-element.2605) | copy-start | bytes 393220 | tf_op jit(solution)/shard_map/while
  548.2 28.3 %collective-permute-start = (bf16[1024,512]{0,1:T(8,128)(2,1)}, bf16[1024,512]{0,1:T(8,128)(2,1)}, u32[]{:S(2)}, u32[]{:S(2)}) collective-permute-start(bf16[1024,512]{0,1:T(8,128)(2,1)} %get-tuple-element.2507), channel_id=1, source_target_pairs={{0,8},{8,16},{16,24},{1,9},{9,17},{17,25},{2,10},{10,18},{18,26},{... | collective-permute-start | bytes 3145736 | tf_op jit(solution)/shard_map/while/body/eval_jaxpr/ppermute | solution.py:16
  586.4 84.9 %copy-start.59 = (f32[2,2,8,1024]{3,2,1,0:T(8,128)S(1)}, f32[2,2,8,1024]{3,2,1,0:T(8,128)}, u32[]{:S(2)}) copy-start(f32[2,2,8,1024]{3,2,1,0:T(8,128)} %get-tuple-element.2605) | copy-start | bytes 393220 | tf_op jit(solution)/shard_map/while
  669.0 28.3 %collective-permute-start = (bf16[1024,512]{0,1:T(8,128)(2,1)}, bf16[1024,512]{0,1:T(8,128)(2,1)}, u32[]{:S(2)}, u32[]{:S(2)}) collective-permute-start(bf16[1024,512]{0,1:T(8,128)(2,1)} %get-tuple-element.2507), channel_id=1, source_target_pairs={{0,8},{8,16},{16,24},{1,9},{9,17},{17,25},{2,10},{10,18},{18,26},{... | collective-permute-start | bytes 3145736 | tf_op jit(solution)/shard_map/while/body/eval_jaxpr/ppermute | solution.py:16
  703.6 1599.8 %reduce-scatter.13.cloned.1.call-start = ((), (), s32[]{:S(2)}) async-start(), calls=%async_computation.8 | async-start | bytes 2621440
  711.3 1599.9 %reduce-scatter.17.cloned.1.call-start = ((), (), s32[]{:S(2)}) async-start(), calls=%async_computation.10 | async-start | bytes 2621440
  756.6 25.0 copy-start.17
  868.0 26.4 %copy-start.18 = (bf16[512,512]{0,1:T(8,128)(2,1)}, bf16[512,512]{0,1:T(8,128)(2,1)S(1)}, u32[]{:S(2)}) copy-start(bf16[512,512]{0,1:T(8,128)(2,1)S(1)} %get-tuple-element.2195) | copy-start | bytes 1572868 | tf_op jit(solution)/shard_map/while/body/eval_jaxpr/cond
  999.4 26.9 %collective-permute-start.1 = (bf16[1024,512]{1,0:T(8,128)(2,1)S(1)}, bf16[1024,512]{1,0:T(8,128)(2,1)S(1)}, u32[]{:S(2)}, u32[]{:S(2)}) collective-permute-start(bf16[1024,512]{1,0:T(8,128)(2,1)S(1)} %get-tuple-element.2541), channel_id=1, source_target_pairs={{8,0},{16,8},{24,16},{9,1},{17,9},{25,17},{10,2},{18,10},{26,18},{... | collective-permute-start | bytes 3145736 | tf_op jit(solution)/shard_map/while/body/eval_jaxpr/ppermute | solution.py:16
  1179.7 26.4 %copy-start.18 = (bf16[512,512]{0,1:T(8,128)(2,1)}, bf16[512,512]{0,1:T(8,128)(2,1)S(1)}, u32[]{:S(2)}) copy-start(bf16[512,512]{0,1:T(8,128)(2,1)S(1)} %get-tuple-element.2195) | copy-start | bytes 1572868 | tf_op jit(solution)/shard_map/while/body/eval_jaxpr/cond
  1311.2 26.0 %collective-permute-start.1 = (bf16[1024,512]{1,0:T(8,128)(2,1)S(1)}, bf16[1024,512]{1,0:T(8,128)(2,1)S(1)}, u32[]{:S(2)}, u32[]{:S(2)}) collective-permute-start(bf16[1024,512]{1,0:T(8,128)(2,1)S(1)} %get-tuple-element.2541), channel_id=1, source_target_pairs={{8,0},{16,8},{24,16},{9,1},{17,9},{25,17},{10,2},{18,10},{26,18},{... | collective-permute-start | bytes 3145736 | tf_op jit(solution)/shard_map/while/body/eval_jaxpr/ppermute | solution.py:16
  1490.6 26.4 %copy-start.18 = (bf16[512,512]{0,1:T(8,128)(2,1)}, bf16[512,512]{0,1:T(8,128)(2,1)S(1)}, u32[]{:S(2)}) copy-start(bf16[512,512]{0,1:T(8,128)(2,1)S(1)} %get-tuple-element.2195) | copy-start | bytes 1572868 | tf_op jit(solution)/shard_map/while/body/eval_jaxpr/cond
  1622.1 25.1 collective-permute-start.1
  1800.6 26.4 %copy-start.18 = (bf16[512,512]{0,1:T(8,128)(2,1)}, bf16[512,512]{0,1:T(8,128)(2,1)S(1)}, u32[]{:S(2)}) copy-start(bf16[512,512]{0,1:T(8,128)(2,1)S(1)} %get-tuple-element.2195) | copy-start | bytes 1572868 | tf_op jit(solution)/shard_map/while/body/eval_jaxpr/cond
  1932.0 24.1 collective-permute-start.1
  2109.6 26.4 %copy-start.18 = (bf16[512,512]{0,1:T(8,128)(2,1)}, bf16[512,512]{0,1:T(8,128)(2,1)S(1)}, u32[]{:S(2)}) copy-start(bf16[512,512]{0,1:T(8,128)(2,1)S(1)} %get-tuple-element.2195) | copy-start | bytes 1572868 | tf_op jit(solution)/shard_map/while/body/eval_jaxpr/cond
  2241.1 23.2 collective-permute-start.1
  2276.7 72.9 %reduce-scatter.19.cloned.1.call-start = ((), (), s32[]{:S(2)}) async-start(), calls=%async_computation.11 | async-start | bytes 2621440
  2286.8 241.4 %all-reduce.4.cloned.1.call-start = ((), (), s32[]{:S(2)}) async-start(), calls=%async_computation.7 | async-start | bytes 16777216 | tf_op jit(solution)/shard_map/psum | solution.py:398
  (457 other events, 2538.9 us)
Sparse Core Ops, SparseCore 0:
  9.8 37.8 all-gather.5
  50.1 35.3 all-gather.3
  87.3 35.1 all-gather.7
  703.7 23.7 reduce-scatter.14
  730.6 35.2 reduce-scatter.12
  2276.8 34.2 reduce-scatter.16
  2314.4 35.1 reduce-scatter.18
  2352.6 175.5 all-reduce.3
where the time goes:
time: 2560 us; the launch traced here: 2540 us
  matrix products  1210 us (47%)
  other arithmetic  542 us (21%)
  waiting for transfers between devices  340 us (13%)
  local copies, waits for them, and re-layouts  329 us (13%)
  loops' own time  68.9 us (3%)
    dot_general x20, matrix products, attend_core_back(): jnp.einsum('qhe,khe->hqk', grad_heads, value_heads, preferred_element_typ...  247 us
    convert_element_type x20, other arithmetic, attend_core_back(): grad_scores = (probs_full * (grad_probs - jnp.sum(grad_probs * probs_full...  191 us
    psum x1, waiting for transfers between devices, local(): summed_bank, summed_gains = lax.psum((ends[1], ends[2]), 'dp')  176 us
    dot_general x20, matrix products, attend_core_back(): jnp.einsum('qhe,khe->hqk', query_heads, key_heads, preferred_element_type...  131 us
    dot_general x20, matrix products, attend_core_back(): jnp.einsum('hqk,khe->qhe', probs, value_heads, preferred_element_type=jnp...  127 us
    dot_general x20, matrix products, attend_core(): jnp.einsum('hqk,khe->qhe', probs, value_heads, preferred_element_type=jnp...  121 us
    dot_general x20, matrix products, attend_core_back(): jnp.einsum('hqk,qhe->khe', probs, grad_heads, preferred_element_type=jnp....  99.9 us
    reduce_sum x20, other arithmetic, attend_core(): summed = jnp.sum(expo, axis=-1, keepdims=True)  87.6 us
  transfers between devices with their start and end apart: 18, of which 10 were waited for; matrix products, arithmetic and copies ran while one was open for 80% of the time, Pallas kernels for 0%

commit v1 on v0

v1 whole, which is shorter than its diff:
```python
import functools

import jax
import jax.numpy as jnp
from jax import lax
from jax.experimental import pallas as pl
from jax.experimental.pallas import tpu as pltpu
from jax.sharding import PartitionSpec as P

HEADS = 8
EPS = 1e-06
BLOCK = 128
NEG = -1e30

bf16 = jnp.bfloat16
f32 = jnp.float32

CORE, FLAG_T, FLAG_M, FIRST, LAST = 0, 1, 2, 3, 4
SELF_LO, SELF_HI, CROSS_LO, CROSS_HI = 8, 16, 24, 32
META = 40


def dot(left, right):
    return jnp.dot(left, right, preferred_element_type=f32)


def dot_nt(left, right):
    return lax.dot_general(left, right, (((1,), (1,)), ((), ())), preferred_element_type=f32)


def dot_tn(left, right):
    return lax.dot_general(left, right, (((0,), (0,)), ((), ())), preferred_element_type=f32)


def exact_nt(left, right):
    return lax.dot_general(
        left, right, (((1,), (1,)), ((), ())), precision=lax.Precision.HIGHEST, preferred_element_type=f32
    )


def exact(left, right):
    return jnp.dot(left, right, precision=lax.Precision.HIGHEST, preferred_element_type=f32)


def norm(x, gain):
    return x * lax.rsqrt(jnp.mean(x * x, axis=-1, keepdims=True) + EPS) * gain


def norm_back(x, gain, grad):
    rate = lax.rsqrt(jnp.mean(x * x, axis=-1, keepdims=True) + EPS)
    scaled = x * rate
    inner = grad * gain
    grad_x = rate * (inner - scaled * jnp.mean(inner * scaled, axis=-1, keepdims=True))
    return grad_x, jnp.sum(grad * scaled, axis=0, keepdims=True)


GELU_A = 0.7978845608028654
GELU_B = 0.044715


def gelu(z):
    return 0.5 * z * (1.0 + jnp.tanh(GELU_A * (z + GELU_B * z * z * z)))


def gelu_both(z):
    square = z * z
    bend = jnp.tanh(GELU_A * z * (1.0 + GELU_B * square))
    half = 0.5 * (1.0 + bend)
    slope = half + 0.5 * z * (1.0 - bend * bend) * (GELU_A * (1.0 + 3.0 * GELU_B * square))
    return z * half, slope


def windows(meta, length):
    wide = length * 5 // 8
    slim = length - wide
    core = meta[CORE]
    return (
        pl.ds(pl.multiple_of(core * slim, BLOCK), wide),
        pl.ds(pl.multiple_of((1 - core) * wide, BLOCK), slim),
    )


def over(meta, flag, length, work):
    main, other = windows(meta, length)
    work(main, True)

    @pl.when(meta[flag] == 1)
    def _():
        work(other, False)


def block(i):
    return pl.ds(pl.multiple_of(i * BLOCK, BLOCK), BLOCK)


def pair_lanes(p):
    return slice(p * BLOCK, (p + 1) * BLOCK)


def two_heads(tile, lane):
    zero = jnp.zeros_like(tile)
    return jnp.concatenate([jnp.where(lane < 64, tile, zero), jnp.where(lane < 64, zero, tile)], axis=0)


def attend_tiles(meta, lo_at, hi_at, low_col, q, k, v, o, lse, cols, scores, peaks, sums):
    pairs = q.shape[1] // BLOCK

    def one_block(i, _):
        first, last = meta[lo_at + i], meta[hi_at + i]

        @pl.when(last > first)
        def _():
            rows = block(i)
            lane = lax.broadcasted_iota(jnp.int32, (BLOCK, BLOCK), 1)
            low = cols[rows, low_col : low_col + 1]
            high = cols[rows, low_col + 1 : low_col + 2]
            peaks[...] = jnp.full(peaks.shape, -jnp.inf, f32)
            sums[...] = jnp.zeros(sums.shape, f32)

            def score(j, _):
                place = lane + j * BLOCK
                bias = jnp.where((place >= low) & (place < high), 0.0, NEG)
                bias = jnp.concatenate([bias, bias], axis=1)
                for p in range(pairs):
                    keys = two_heads(k[block(j), pair_lanes(p)], lane)
                    tile = dot_nt(q[rows, pair_lanes(p)], keys) + bias
                    scores[j - first, p] = tile
                    peaks[p] = jnp.maximum(peaks[p], tile)
                return 0

            lax.fori_loop(first, last, score, 0)
            for p in range(pairs):
                for e in range(2):
                    lanes = slice(e * BLOCK, (e + 1) * BLOCK)
                    top = jnp.max(peaks[p, :, lanes], axis=-1, keepdims=True)
                    peaks[p, :, lanes] = jnp.broadcast_to(top, (BLOCK, BLOCK))

            def mix(j, _):
                ones = jnp.where(lane < 64, 1.0, 0.0).astype(bf16)
                marks = jnp.concatenate([ones, 1 - ones], axis=0)
                for p in range(pairs):
                    weights = jnp.exp(scores[j - first, p] - peaks[p]).astype(bf16)
                    values = two_heads(v[block(j), pair_lanes(p)], lane)
                    sums[p] += dot(weights, jnp.concatenate([values, marks], axis=1))
                return 0

            lax.fori_loop(first, last, mix, 0)
            gathered = jnp.zeros((BLOCK, BLOCK), f32)
            for p in range(pairs):
                total = sums[p, :, BLOCK:]
                o[rows, pair_lanes(p)] = (sums[p, :, :BLOCK] / total).astype(bf16)
                top = jnp.where(lane < 64, peaks[p, :, :BLOCK], peaks[p, :, BLOCK:])
                gathered = jnp.where(lane % 64 // 16 == p, top + jnp.log(total), gathered)
            turned = gathered.T
            for p in range(pairs):
                for e in range(2):
                    lse[2 * p + e : 2 * p + e + 1, rows] = turned[e * 64 + p * 16 : e * 64 + p * 16 + 1, :]

        return 0

    lax.fori_loop(meta[FIRST], meta[LAST], one_block, 0)


def attend_tiles_back(
    meta, lo_at, hi_at, low_row, q, k, v, lse, delta, do, info, dq, dk, dv, both_q, both_o, dq_sum
):
    pairs = q.shape[1] // BLOCK

    def one_block(i, _):
        first, last = meta[lo_at + i], meta[hi_at + i]

        @pl.when(last > first)
        def _():
            rows = block(i)
            lane = lax.broadcasted_iota(jnp.int32, (BLOCK, BLOCK), 1)
            slot = lax.broadcasted_iota(jnp.int32, (BLOCK, BLOCK), 0)
            low = info[low_row : low_row + 1, rows]
            high = info[low_row + 1 : low_row + 2, rows]
            dq_sum[...] = jnp.zeros(dq_sum.shape, f32)
            for p in range(pairs):
                both_q[p] = two_heads(q[rows, pair_lanes(p)], lane)
                both_o[p] = two_heads(do[rows, pair_lanes(p)], lane)

            def tile(j, _):
                place = slot + j * BLOCK
                bias = jnp.where((place >= low) & (place < high), 0.0, NEG)
                bias = jnp.concatenate([bias, bias], axis=1)
                for p in range(pairs):
                    lanes = pair_lanes(p)
                    keys, values = k[block(j), lanes], v[block(j), lanes]
                    queries, grads = both_q[p], both_o[p]
                    log_total = jnp.concatenate([lse[2 * p : 2 * p + 1, rows], lse[2 * p + 1 : 2 * p + 2, rows]], axis=1)
                    change = jnp.concatenate([delta[2 * p : 2 * p + 1, rows], delta[2 * p + 1 : 2 * p + 2, rows]], axis=1)
                    probs = jnp.exp(dot_nt(keys, queries) + bias - log_total)
                    grad_scores = (probs * (dot_nt(values, grads) - change)).astype(bf16)
                    dv[block(j), lanes] += dot(probs.astype(bf16), grads)
                    dk[block(j), lanes] += dot(grad_scores, queries)
                    mixed = dot_tn(grad_scores, keys)
                    dq_sum[:, lanes] += jnp.where(lane < 64, mixed[:BLOCK], mixed[BLOCK:])
                return 0

            lax.fori_loop(first, last, tile, 0)
            dq[rows, :] = (dq_sum[...] * 0.125).astype(bf16)

        return 0

    lax.fori_loop(meta[FIRST], meta[LAST], one_block, 0)


def attention_forward_kernel(
    meta, x, mem, w, gain, go, cols, q1, k1, v1, o1, l1, mid, q2, k2, v2, o2, l2, out, scores, peaks, sums
):
    length = x.shape[0]

    def self_in(rows, _):
        a = norm(x[rows, :].astype(f32), gain[0:1, :]).astype(bf16)
        q1[rows, :] = (dot(a, w[0]) * 0.125).astype(bf16)
        k1[rows, :] = dot(a, w[1]).astype(bf16)
        v1[rows, :] = dot(a, w[2]).astype(bf16)
        o1[rows, :] = jnp.zeros((rows.size, x.shape[1]), bf16)

    over(meta, FLAG_T, length, self_in)

    def memory_in(rows, _):
        source = mem[rows, :]
        k2[rows, :] = dot(source, w[5]).astype(bf16)
        v2[rows, :] = dot(source, w[6]).astype(bf16)

    over(meta, FLAG_M, length, memory_in)
    l1[...] = jnp.zeros(l1.shape, f32)
    l2[...] = jnp.zeros(l2.shape, f32)
    attend_tiles(meta, SELF_LO, SELF_HI, 0, q1, k1, v1, o1, l1, cols, scores, peaks, sums)

    def cross_in(rows, _):
        state = x[rows, :].astype(f32) + go[rows, 0:1] * dot(o1[rows, :], w[3])
        mid[rows, :] = state
        a = norm(state, gain[1:2, :]).astype(bf16)
        q2[rows, :] = (dot(a, w[4]) * 0.125).astype(bf16)
        o2[rows, :] = jnp.zeros((rows.size, x.shape[1]), bf16)

    over(meta, FLAG_T, length, cross_in)
    attend_tiles(meta, CROSS_LO, CROSS_HI, 2, q2, k2, v2, o2, l2, cols, scores, peaks, sums)

    def finish(rows, _):
        out[rows, :] = (mid[rows, :] + go[rows, 0:1] * dot(o2[rows, :], w[7])).astype(bf16)

    over(meta, FLAG_T, length, finish)


def attention_backward_kernel(
    meta, x, mem, w, gain, go, info, q1, k1, v1, o1, l1, mid, q2, k2, v2, o2, l2, dh, dmem_in,
    dx, dmem, dw, dgain,
    dstate, do, dq, dk, dv, dkb, dvb, delta, both_q, both_o, dq_sum, acc, heads,
):
    length, width = x.shape
    row_of = lax.broadcasted_iota(jnp.int32, (HEADS, width), 0)
    lane_of = lax.broadcasted_iota(jnp.int32, (HEADS, width), 1)
    heads[...] = (lane_of // (width // HEADS) == row_of).astype(bf16)
    dk[...] = jnp.zeros(dk.shape, f32)
    dv[...] = jnp.zeros(dv.shape, f32)
    delta[...] = jnp.zeros(delta.shape, f32)

    def weight_grad(index, flag, left, right):
        def part(rows, fresh):
            term = dot_tn(left(rows), right(rows))
            acc[...] = term if fresh else acc[...] + term

        over(meta, flag, length, part)
        dw[index] = acc[...].astype(bf16)

    def begin(grad_of, o, out_weight):
        def part(rows, _):
            dy = (go[rows, 0:1] * grad_of(rows)).astype(bf16)
            grad = dot_nt(dy, w[out_weight]).astype(bf16)
            do[rows, :] = grad
            product = grad.astype(f32) * o[rows, :].astype(f32)
            high = product.astype(bf16)
            rest = (product - high.astype(f32)).astype(bf16)
            delta[:, rows] = dot_nt(heads[...], high) + dot_nt(heads[...], rest)
            dq[rows, :] = jnp.zeros((rows.size, width), bf16)

        over(meta, FLAG_T, length, part)
        weight_grad(out_weight, FLAG_T, lambda rows: o[rows, :], lambda rows: (go[rows, 0:1] * grad_of(rows)).astype(bf16))

    def top_grad(rows):
        return dh[rows, :].astype(f32)

    begin(top_grad, o2, 7)
    attend_tiles_back(
        meta, CROSS_LO, CROSS_HI, 2, q2, k2, v2, l2, delta, do, info, dq, dk, dv, both_q, both_o, dq_sum
    )

    dmem[...] = dmem_in[...]

    def memory_out(rows, _):
        grad_k, grad_v = dk[rows, :].astype(bf16), dv[rows, :].astype(bf16)
        dkb[rows, :] = grad_k
        dvb[rows, :] = grad_v
        dmem[rows, :] += dot_nt(grad_k, w[5]) + dot_nt(grad_v, w[6])

    over(meta, FLAG_M, length, memory_out)
    weight_grad(5, FLAG_M, lambda rows: mem[rows, :], lambda rows: dkb[rows, :])
    weight_grad(6, FLAG_M, lambda rows: mem[rows, :], lambda rows: dvb[rows, :])

    def cross_out(rows, fresh):
        state = mid[rows, :]
        grad_x, grad_gain = norm_back(state, gain[1:2, :], dot_nt(dq[rows, :], w[4]))
        dstate[rows, :] = top_grad(rows) + grad_x
        dgain[1:2, :] = grad_gain if fresh else dgain[1:2, :] + grad_gain

    over(meta, FLAG_T, length, cross_out)
    weight_grad(4, FLAG_T, lambda rows: norm(mid[rows, :], gain[1:2, :]).astype(bf16), lambda rows: dq[rows, :])

    dk[...] = jnp.zeros(dk.shape, f32)
    dv[...] = jnp.zeros(dv.shape, f32)
    begin(lambda rows: dstate[rows, :], o1, 3)
    attend_tiles_back(
        meta, SELF_LO, SELF_HI, 0, q1, k1, v1, l1, delta, do, info, dq, dk, dv, both_q, both_o, dq_sum
    )

    def self_out(rows, fresh):
        grad_k, grad_v = dk[rows, :].astype(bf16), dv[rows, :].astype(bf16)
        dkb[rows, :] = grad_k
        dvb[rows, :] = grad_v
        da = dot_nt(dq[rows, :], w[0]) + dot_nt(grad_k, w[1]) + dot_nt(grad_v, w[2])
        grad_x, grad_gain = norm_back(x[rows, :].astype(f32), gain[0:1, :], da)
        dx[rows, :] = (dstate[rows, :] + grad_x).astype(bf16)
        dgain[0:1, :] = grad_gain if fresh else dgain[0:1, :] + grad_gain

    over(meta, FLAG_T, length, self_out)

    def normed(rows):
        return norm(x[rows, :].astype(f32), gain[0:1, :]).astype(bf16)

    weight_grad(0, FLAG_T, normed, lambda rows: dq[rows, :])
    weight_grad(1, FLAG_T, normed, lambda rows: dkb[rows, :])
    weight_grad(2, FLAG_T, normed, lambda rows: dvb[rows, :])


def exit_part(layer, vector, frows, rows, target_row, halt, exit_grad, fresh, sentences):
    factor = layer.shape[1] ** (-0.5)
    vectors = jnp.broadcast_to(vector, (8, layer.shape[1]))
    score = jax.nn.sigmoid(exact_nt(vectors, layer) * factor)
    halt[:, rows] = score
    weight = frows[0:1, rows] * (score - frows[target_row : target_row + 1, rows]) / sentences
    term = exact(weight, layer)[0:1] * factor
    exit_grad[...] = term if fresh else exit_grad[...] + term


def dense_forward_kernel(sentences, meta, x, w, gain, frows, out, halt, exit_grad):
    length = x.shape[0]
    parts = w.shape[0] // 2

    def part(rows, fresh):
        state = x[rows, :].astype(f32)
        a = norm(state, gain[0:1, :]).astype(bf16)
        branch = jnp.zeros(state.shape, f32)
        for j in range(parts):
            branch = branch + dot(gelu(dot(a, w[j])).astype(bf16), w[parts + j])
        layer = state + branch
        out[rows, :] = layer.astype(bf16)
        exit_part(layer, gain[1:2, :], frows, rows, 1, halt, exit_grad, fresh, sentences)

    over(meta, FLAG_T, length, part)


def dense_backward_kernel(sentences, final, meta, x, w, gain, go, frows, dh, dx, dw, dgain, *rest):
    if final:
        out, halt, exit_grad, acc = rest
    else:
        (acc,) = rest
    length, width = x.shape
    parts = w.shape[0] // 2

    def part(rows, fresh):
        state = x[rows, :].astype(f32)
        a = norm(state, gain[0:1, :]).astype(bf16)
        dy = (go[rows, 0:1] * dh[rows, :].astype(f32)).astype(bf16)
        branch = jnp.zeros(state.shape, f32)
        da = jnp.zeros(state.shape, f32)
        for j in range(parts):
            active, slope = gelu_both(dot(a, w[j]))
            active = active.astype(bf16)
            if final:
                branch = branch + dot(active, w[parts + j])
            dhidden = (slope * dot_nt(dy, w[parts + j])).astype(bf16)
            da = da + dot_nt(dhidden, w[j])
            up, down = dot_tn(a, dhidden), dot_tn(active, dy)
            acc[j] = up if fresh else acc[j] + up
            acc[parts + j] = down if fresh else acc[parts + j] + down
        grad_x, grad_gain = norm_back(state, gain[0:1, :], da)
        dx[rows, :] = (dh[rows, :].astype(f32) + grad_x).astype(bf16)
        dgain[...] = grad_gain if fresh else dgain[...] + grad_gain
        if final:
            layer = state + go[rows, 0:1] * branch
            out[rows, :] = layer.astype(bf16)
            exit_part(layer, gain[1:2, :], frows, rows, 2, halt, exit_grad, fresh, sentences)

    over(meta, FLAG_T, length, part)
    for j in range(2 * parts):
        dw[j] = acc[j].astype(bf16)


VMEM = pl.BlockSpec(memory_space=pltpu.VMEM)
SMEM = pl.BlockSpec(memory_space=pltpu.SMEM)


def run(kernel, outs, scratch, name, flops, *args):
    return pl.pallas_call(
        kernel,
        out_shape=[jax.ShapeDtypeStruct(shape, dtype) for shape, dtype in outs],
        in_specs=[SMEM] + [VMEM] * (len(args) - 1),
        out_specs=[VMEM] * len(outs),
        scratch_shapes=[pltpu.VMEM(shape, dtype) for shape, dtype in scratch],
        compiler_params=pltpu.CompilerParams(vmem_limit_bytes=60 * 2**20),
        cost_estimate=pl.CostEstimate(flops=flops, bytes_accessed=20 * 2**20, transcendentals=0),
        name=name,
    )(*args)


def attention_forward(meta, x, mem, w, gain, go, cols, name):
    length, width = x.shape
    wide = ((length, width), bf16)
    logs = ((HEADS, length), f32)
    pairs = width // BLOCK
    tile = ((pairs, BLOCK, 2 * BLOCK), f32)
    return run(
        attention_forward_kernel,
        [wide, wide, wide, wide, logs, ((length, width), f32), wide, wide, wide, wide, logs, wide],
        [((length // BLOCK,) + tile[0], f32), tile, tile],
        name, 6 * 10**9, meta, x, mem, w, gain, go, cols,
    )


def attention_backward(meta, x, mem, w, gain, go, info, saved, dh, dmem, name):
    length, width = x.shape
    pairs = width // BLOCK
    wide, full = ((length, width), bf16), ((length, width), f32)
    both = ((pairs, 2 * BLOCK, BLOCK), bf16)
    return run(
        attention_backward_kernel,
        [wide, full, (w.shape, bf16), ((2, width), f32)],
        [full, wide, wide, full, full, wide, wide, ((HEADS, length), f32), both, both,
         ((BLOCK, width), f32), ((width, width), f32), ((HEADS, width), bf16)],
        name, 12 * 10**9, meta, x, mem, w, gain, go, info, *saved, dh, dmem,
    )


def dense_forward(meta, x, w, gain, frows, sentences, name):
    length, width = x.shape
    return run(
        functools.partial(dense_forward_kernel, sentences),
        [((length, width), bf16), ((8, length), f32), ((1, width), f32)], [],
        name, 4 * 10**9, meta, x, w, gain, frows,
    )


def dense_backward(meta, x, w, gain, go, frows, dh, sentences, final, name):
    length, width = x.shape
    outs = [((length, width), bf16), (w.shape, bf16), ((1, width), f32)]
    if final:
        outs += [((length, width), bf16), ((8, length), f32), ((1, width), f32)]
    return run(
        functools.partial(dense_backward_kernel, sentences, final), outs, [(w.shape, f32)],
        name, 8 * 10**9, meta, x, w, gain, go, frows, dh,
    )


def plan(core, seg, pad, mseg, mmask, depths):
    length, slots, sentences = seg.shape[0], mseg.shape[0], depths.shape[0]
    numbers = jnp.arange(sentences)
    place = jnp.arange(length)
    mine = (seg[:, None] == numbers[None, :]).astype(jnp.int32)

    def of_token(table):
        return jnp.sum(mine * table[None, :], axis=1)

    starts = jnp.sum((seg[:, None] < numbers[None, :]).astype(jnp.int32), axis=0)
    filled = jnp.sum(pad)
    memory_starts = jnp.sum((mseg[:, None] < numbers[None, :]).astype(jnp.int32), axis=0)
    memory_stops = jnp.sum((mseg[:, None] <= numbers[None, :]).astype(jnp.int32), axis=0)
    memory_stops = jnp.minimum(memory_stops, jnp.sum(mmask))
    low = of_token(starts)
    high = jnp.where(pad == 1, jnp.minimum(place, filled - 1), place) + 1
    cross_low = jnp.where(pad == 0, 0, of_token(memory_starts))
    cross_high = jnp.where(pad == 0, slots, of_token(memory_stops))
    depth = of_token(depths)
    keep = depth == 2

    away = jnp.abs(starts[1:] - length // 2)
    cut = jnp.min(jnp.where(away == jnp.min(away), starts[1:], length))
    owned = jnp.where(core == 0, place < cut, place >= cut)
    blocks = length // BLOCK
    begin = jnp.where(core == 0, 0, cut // BLOCK)
    end = jnp.where(core == 0, (cut + BLOCK - 1) // BLOCK, blocks)
    wide = length * 5 // 8

    def outside(from_place, to_place):
        return jnp.where(core == 0, to_place > wide, from_place < length - wide)

    def span(lows, highs, used):
        lows = jnp.min(jnp.where(used, lows, length).reshape(blocks, BLOCK), axis=1)
        highs = jnp.max(jnp.where(used, highs, 0).reshape(blocks, BLOCK), axis=1)
        return jnp.minimum(lows, highs) // BLOCK, (highs + BLOCK - 1) // BLOCK

    def steer(used):
        self_span, cross_span = span(low, high, used), span(cross_low, cross_high, used)
        flag_t = outside(begin * BLOCK, end * BLOCK)
        flag_m = outside(
            jnp.min(jnp.where(used, cross_low, slots)), jnp.max(jnp.where(used, cross_high, 0))
        )
        head = jnp.stack([core, flag_t, flag_m, begin, end, 0, 0, 0]).astype(jnp.int32)
        return jnp.concatenate([head, *self_span, *cross_span]).astype(jnp.int32)

    cols = jnp.pad(jnp.stack([low, high, cross_low, cross_high], axis=1), ((0, 0), (0, 4)))
    info = jnp.pad(jnp.stack([low, high, cross_low, cross_high]), ((0, 4), (0, 0)))
    onward = jnp.broadcast_to(keep.astype(f32)[:, None], (length, 8))
    counted = pad.astype(f32) * owned.astype(f32)
    frows = jnp.stack([counted, (depth == 1).astype(f32), jnp.ones_like(counted)])
    frows = jnp.pad(frows, ((0, 5), (0, 0)))
    return steer(owned), steer(owned & keep), cols, info, onward, frows, owned


def row_forward_backward(core, x, mem, cotangent, w, gains, ints, sentences):
    first, second, cols, info, keep, frows, owned = plan(core, *ints)
    length, width = x.shape
    every = jnp.ones_like(keep)
    cotangent = jnp.where(owned[:, None], cotangent, 0).astype(bf16)
    *saved0, zero = attention_forward(first, x, mem, w[0], gains[0], every, cols, "attend_zero")
    one, halt0, exit0 = dense_forward(first, zero, w[1], gains[1], frows, sentences, "dense_one")
    *saved2, two = attention_forward(second, one, mem, w[2], gains[2], keep, cols, "attend_two")
    dtwo, dw3, dgain3, states, halt1, exit1 = dense_backward(
        first, two, w[3], gains[3], keep, frows, cotangent, sentences, True, "dense_three"
    )
    nothing = jnp.zeros((length, width), f32)
    done, dmem, dw2, dgain2 = attention_backward(
        second, one, mem, w[2], gains[2], keep, info, saved2, dtwo, nothing, "attend_two_back"
    )
    dzero, dw1, dgain1 = dense_backward(
        first, zero, w[1], gains[1], every, frows, done, sentences, False, "dense_one_back"
    )
    dx, dmem, dw0, dgain0 = attention_backward(
        first, x, mem, w[0], gains[0], every, info, saved0, dzero, dmem, "attend_zero_back"
    )
    halt = jnp.where(owned[None, :], jnp.stack([halt0[0], halt1[0]]), 0)
    dgains = jnp.stack(
        [dgain0, jnp.concatenate([dgain1, exit0]), dgain2, jnp.concatenate([dgain3, exit1])]
    )
    states = jnp.where(owned[:, None], states, 0)
    dx = jnp.where(owned[:, None], dx, 0)
    return states, halt, dx, dmem, [dw0, dw1, dw2, dw3], dgains


def swap_cores(value):
    count = lax.axis_size("dp")
    return lax.ppermute(value, "dp", [(i, i ^ 1) for i in range(count)])


def local(
    states_in, memory, cotangent, weight_bank, gain_bank, segments, pad_mask, memory_segments, memory_mask, exit_depths
):
    section = lax.axis_index("section")
    sections = lax.axis_size("section")
    core = lax.axis_index("dp") % 2
    micro = states_in.shape[0]
    sentences = exit_depths.shape[1]
    holder = section // micro == core

    def whole_row(shares):
        gathered = lax.all_gather(shares, "section", axis=2, tiled=True)
        own = lax.dynamic_index_in_dim(gathered, section % micro, 0, keepdims=False)
        return jnp.where(holder, own, swap_cores(own))

    def row_of(ints):
        own = lax.dynamic_index_in_dim(ints, section % micro, 0, keepdims=False)
        return jnp.where(holder, own, swap_cores(own))

    x, mem, top = whole_row(states_in), whole_row(memory), whole_row(cotangent)
    ints = [row_of(t) for t in (segments, pad_mask, memory_segments, memory_mask, exit_depths)]
    w = lax.all_gather(weight_bank[0], "section")
    gains = lax.all_gather(gain_bank[0], "section")
    states, halt, dx, dmem, dw, dgains = row_forward_backward(
        core, x, mem, top, [w[i] for i in range(sections)], gains, ints, sentences
    )

    def to_shares(value, axis):
        value = value.astype(bf16)
        both = value.astype(f32) + swap_cores(value).astype(f32)
        both = jnp.where(holder, both, 0).astype(bf16)
        slots = jnp.stack([jnp.where(section % micro == i, both, 0) for i in range(micro)])
        return lax.psum_scatter(slots, "section", scatter_dimension=axis + 1, tiled=True)

    bank = lax.psum_scatter(jnp.stack(dw), "section", scatter_dimension=0, tiled=True)
    bank = lax.psum(bank.astype(f32), "dp")
    gain_sum = lax.psum_scatter(dgains, "section", scatter_dimension=0, tiled=True)
    gain_sum = lax.psum(gain_sum, "dp")
    return (
        to_shares(states, 1),
        to_shares(halt, 1).astype(f32),
        to_shares(dx, 1).astype(f32),
        to_shares(dmem, 1).astype(f32),
        bank,
        gain_sum,
    )


def solution(mesh):
    rows = P("dp", None, "section")
    return jax.shard_map(
        local,
        mesh=mesh,
        in_specs=(
            rows, rows, rows, P("section", None, None, None), P("section", None, None),
            P("dp", None), P("dp", None), P("dp", None), P("dp", None), P("dp", None),
        ),
        out_specs=(rows, rows, rows, rows, P("section", None, None, None), P("section", None, None)),
        check_vma=False,
    )
```

time: 2560 us -> 1000 us (0.39)
  matrix products: 1210 us -> 0 us
  other arithmetic: 542 us -> 34.9 us
  local copies, waits for them, and re-layouts: 329 us -> 63.2 us
  blocking collectives: 14.2 us -> 194 us
  Pallas kernels: 0 us -> 146 us
  waiting for transfers between devices: 340 us -> 458 us
  loops' own time: 68.9 us -> 0 us
  starting transfers between devices: 19 us -> 85.3 us
    dot_general x310 -> x0, matrix products: 1210 us -> none  [the longest x20 247 us: attend_core_back(): jnp.einsum('qhe,khe->hqk', grad_heads, value_heads, preferred_element_typ...]
    convert_element_type x45 -> x6, other arithmetic: 222 us -> 5.55 us  [the longest x2 2.86 us: to_shares(): value = value.astype(bf16)]
    unnamed x12 -> x14, waiting for transfers between devices: 42.7 us -> 221 us
    psum x1 -> x0, waiting for transfers between devices: 176 us -> none  [local(): summed_bank, summed_gains = lax.psum((ends[1], ends[2]), 'dp')]
    all_gather x3 -> x4, waiting for transfers between devices: 73.1 us -> 231 us  [the longest x1 151 us: local(): w = lax.all_gather(weight_bank[0], 'section')]
    psum x1, blocking collectives: 14.2 us -> 170 us  [local(): bank = lax.psum(bank.astype(f32), 'dp')]
    pallas_call x0 -> x7, Pallas kernels: none -> 146 us  [run(): pl.pallas_call(kernel, out_shape=[jax.ShapeDtypeStruct(shape, dtype) for...]
    reduce_sum x45 -> x5, other arithmetic: 91.5 us -> 1.65 us  [the longest x1 0.63 us: plan(): memory_stops = jnp.minimum(memory_stops, jnp.sum(mmask))]
  transfers between devices with their start and end apart: 18 -> 21, of which waited for: 10 -> 10; matrix products, arithmetic and copies ran while one was open for 80% -> 8% of each run, Pallas kernels for 0% -> 0%
where the time goes in v1:
time: 1000 us
  waiting for transfers between devices  458 us (46%)
  blocking collectives  194 us (19%)
  Pallas kernels  146 us (15%)
  starting transfers between devices  85.3 us (9%)
  local copies, waits for them, and re-layouts  63.2 us (6%)
  other arithmetic  34.9 us (3%)
  between operations  21.3 us (2%)
    unnamed x14, waiting for transfers between devices  221 us
    psum x1, blocking collectives, local(): bank = lax.psum(bank.astype(f32), 'dp')  170 us
    all_gather x1, waiting for transfers between devices, local(): w = lax.all_gather(weight_bank[0], 'section')  151 us
    pallas_call x7, Pallas kernels, run(): pl.pallas_call(kernel, out_shape=[jax.ShapeDtypeStruct(shape, dtype) for...  146 us
    ppermute x12, starting transfers between devices, swap_cores(): return lax.ppermute(value, 'dp', [(i, i ^ 1) for i in range(count)])  84.7 us
    all_gather x3, waiting for transfers between devices, whole_row(): gathered = lax.all_gather(shares, 'section', axis=2, tiled=True)  79.2 us
    unnamed x58, local copies, waits for them, and re-layouts  35.9 us
  transfers between devices with their start and end apart: 21, of which 10 were waited for; matrix products, arithmetic and copies ran while one was open for 8% of the time, Pallas kernels for 0%

profile of v1, /device:TPU:0, one launch (start us, length us, event | category | flops | bytes accessed | tf_op | source)
XLA Modules:
  0.0 1002.5 jit_solution(1004214504270624792)
XLA Ops:
  12.1 9.2 all_gather.18
  35.7 12.0 %all-gather.5.cloned.1.call-done = bf16[2,1024,512]{2,1,0:T(8,128)(2,1)} async-done(((bf16[2,1024,128]{2,1,0:T(8,128)(2,1)}), bf16[2,1024,512]{2,1,0:T(8,128)(2,1)}) %all-gather.5.cloned.1.call-update) | async-done | bytes 2097168 | tf_op jit(solution)/shard_map/all_gather | solution.py:570
  47.8 2.3 dynamic-slice_bitcast_fusion.2
  50.7 34.1 %all-gather.7.cloned.1.call-done = bf16[2,1024,512]{2,1,0:T(8,128)(2,1)} async-done(((bf16[2,1024,128]{2,1,0:T(8,128)(2,1)}), bf16[2,1024,512]{2,1,0:T(8,128)(2,1)}) %all-gather.7.cloned.1.call-update) | async-done | bytes 2097168 | tf_op jit(solution)/shard_map/all_gather | solution.py:570
  84.8 2.3 dynamic-slice_bitcast_fusion.1
  88.8 33.1 %all-gather.11.cloned.1.call-done = bf16[2,1024,512]{2,1,0:T(8,128)(2,1)} async-done(((bf16[2,1024,128]{2,1,0:T(8,128)(2,1)}), bf16[2,1024,512]{2,1,0:T(8,128)(2,1)}) %all-gather.11.cloned.1.call-update) | async-done | bytes 2097168 | tf_op jit(solution)/shard_map/all_gather | solution.py:570
  129.7 151.3 %all-gather.9.cloned.1.call-done = bf16[4,8,512,512]{3,2,1,0:T(8,128)(2,1)} async-done(((bf16[1,8,512,512]{3,2,1,0:T(8,128)(2,1)}), bf16[4,8,512,512]{3,2,1,0:T(8,128)(2,1)}) %all-gather.9.cloned.1.call-update) | async-done | bytes 16777232 | tf_op jit(solution)/shard_map/all_gather | solution.py:580
  281.0 12.3 %slice_bitcast_fusion = (bf16[8,512,512]{2,1,0:T(8,128)(2,1)}, bf16[8,512,512]{2,1,0:T(8,128)(2,1)}, bf16[8,512,512]{2,1,0:T(8,128)(2,1)}, bf16[8,512,512]{2,1,0:T(8,128)(2,1)}) fusion(bf16[4,8,512,512]{3,2,1,0:T(8,128)(2,1)} %all-gather.9.cloned.1.call-done), kind=kLoop, calls=%fused_computation.1 | loop fusion | bytes 33554432 | tf_op jit(solution)/shard_map/squeeze | solution.py:583
  294.1 22.4 %attend_zero.1 = (bf16[1024,512]{1,0:T(8,128)(2,1)}, bf16[1024,512]{1,0:T(8,128)(2,1)}, bf16[1024,512]{1,0:T(8,128)(2,1)}, bf16[1024,512]{1,0:T(8,128)(2,1)}, f3...) custom-call(s32[40]{0:T(128)} %concatenate.12.meta, ...), custom_call_target="tpu_custom_call" | custom-call | flops 6000000000 | bytes 20971520 | tf_op jit(solution)/shard_map/attend_zero/pallas_call | solution.py:409
  316.5 8.3 dense_one.1
  325.8 15.9 %attend_two.1 = (bf16[1024,512]{1,0:T(8,128)(2,1)}, bf16[1024,512]{1,0:T(8,128)(2,1)}, bf16[1024,512]{1,0:T(8,128)(2,1)}, bf16[1024,512]{1,0:T(8,128)(2,1)}, f32...) custom-call(s32[40]{0:T(128)} %concatenate.13.meta, ...), custom_call_target="tpu_custom_call" | custom-call | flops 6000000000 | bytes 20971520 | tf_op jit(solution)/shard_map/attend_two/pallas_call | solution.py:409
  341.7 17.2 %dense_three.1 = (bf16[1024,512]{1,0:T(8,128)(2,1)}, bf16[8,512,512]{2,1,0:T(8,128)(2,1)}, f32[1,512]{1,0:T(1,128)}, bf16[1024,512]{1,0:T(8,128)(2,1)}, f32[8,1024]{1,0:T(8,128)}, /*index=5*/f32[1,512]{1,0:T(1,128)}) custom-call(s32[40]{0:T(128)} %concatenate.12.meta, bf16[1024,512]{1,0:T(8,128)(2,1)} %get-tuple-element.52.x, ...), custom_call_target="tpu_custom_call" | custom-call | flops 8000000000 | bytes 20971520 | tf_op jit(solution)/shard_map/dense_three/pallas_call | solution.py:409
  360.5 28.5 %attend_two_back.1 = (bf16[1024,512]{1,0:T(8,128)(2,1)}, f32[1024,512]{1,0:T(8,128)}, bf16[8,512,512]{2,1,0:T(8,128)(2,1)}, f32[2,512]{1,0:T(2,128)}) custom-call(s32[40]{0:T(128)} %concatenate.13.meta, bf16[1024,512]{1,0:T(8,128)(2,1)} %get-tuple-element.51.x, bf16[1024,512]{1,0:T(8,128)(2,1)} %broadcast_select_fusion.2.mem, ...), custom_call_target="tpu_custom_call" | custom-call | flops 12000000000 | bytes 20971520 | tf_op jit(solution)/shard_map/attend_two_back/pallas_call | solution.py:409
  389.0 14.7 %dense_one_back.1 = (bf16[1024,512]{1,0:T(8,128)(2,1)}, bf16[8,512,512]{2,1,0:T(8,128)(2,1)}, f32[1,512]{1,0:T(1,128)}) custom-call(s32[40]{0:T(128)} %concatenate.12.meta, bf16[1024,512]{1,0:T(8,128)(2,1)} %get-tuple-element.50.x, bf16[8,512,512]{2,1,0:T(8,128)(2,1)} %get-tuple-element.130.w, f32[2,512]{1,0:T(2,128)} %get-tuple-element.140.gain, ...), custom_call_target="tpu_custom_call" | custom-call | flops 8000000000 | bytes 20971520 | tf_op jit(solution)/shard_map/dense_one_back/pallas_call | solution.py:409
  403.8 39.4 %attend_zero_back.1 = (bf16[1024,512]{1,0:T(8,128)(2,1)}, f32[1024,512]{1,0:T(8,128)}, bf16[8,512,512]{2,1,0:T(8,128)(2,1)}, f32[2,512]{1,0:T(2,128)}) custom-call(s32[40]{0:T(128)} %concatenate.12.meta, bf16[1024,512]{1,0:T(8,128)(2,1)} %broadcast_select_fusion.3.x, bf16[1024,512]{1,0:T(8,128)(2,1)} %broadcast_select_fusion.2.mem, ...), custom_call_target="tpu_custom_call" | custom-call | flops 12000000000 | bytes 20971520 | tf_op jit(solution)/shard_map/attend_zero_back/pallas_call | solution.py:409
  443.2 2.8 convert_element_type.135
  446.0 82.4 %collective-permute-start.11 = (bf16[1024,512]{1,0:T(8,128)(2,1)}, bf16[1024,512]{1,0:T(8,128)(2,1)}, u32[]{:S(2)}, u32[]{:S(2)}) collective-permute-start(bf16[1024,512]{1,0:T(8,128)(2,1)} %convert_element_type.135), channel_id=1, source_target_pairs={{0,1},{1,0},{2,3},{3,2},{4,5},{5,4},{6,7},{7,6},{8,9},{9,8},{10,11... | collective-permute-start | bytes 3145736 | tf_op jit(solution)/shard_map/ppermute | solution.py:556
  533.0 1.7 select_bitcast_fusion.1
  535.0 4.1 copy.28
  539.0 3.5 copy.32
  544.5 2.5 collective-permute-done.10
  547.8 4.1 copy.26
  551.8 3.6 copy.31
  555.6 2.5 collective-permute-done.8
  558.9 4.1 copy.22
  562.9 3.5 copy.30
  566.5 14.1 %pad_maximum_fusion = bf16[4,8,512,512]{3,2,1,0:T(8,128)(2,1)} fusion(bf16[1,8,512,512]{3,2,1,0:T(8,128)(2,1)} %bitcast.123, bf16[1,8,512,512]{3,2,1,0:T(8,128)(2,1)} %bitcast.124, bf16[1,8,512,512]{3,2,1,0:T(8,128)(2,1)} %bitcast.125, bf16[1,8,512,512]{3,2,1,0:T(8,128)(2,1)} %bitcast.126), kind=kLoop, calls=%fused_computation | loop fusion | flops 25165824 | bytes 33554432 | tf_op jit(solution)/shard_map/stack | solution.py:593
  581.9 14.0 %all-reduce.4 = f32[4,2,512]{2,1,0:T(2,128)S(1)} all-reduce(f32[4,2,512]{2,1,0:T(2,128)S(1)} %pad_maximum_fusion.4), channel_id=7, replica_groups=mesh['section'=4,'dp'=8] {'section'}, use_global_device_ids=true, to_apply=%region_29.30.clone | all-reduce | flops 4096 | bytes 32768
  601.2 28.4 %reduce-scatter.20.cloned.1.call-done = bf16[128,2048]{1,0:T(8,128)(2,1)} async-done(((bf16[512,2048]{1,0:T(8,128)(2,1)}), bf16[128,2048]{1,0:T(8,128)(2,1)}) %reduce-scatter.20.cloned.1.call-update) | async-done | bytes 524304
  632.6 35.4 %reduce-scatter.16.cloned.1.call-done = bf16[128,2048]{1,0:T(8,128)(2,1)} async-done(((bf16[512,2048]{1,0:T(8,128)(2,1)}), bf16[128,2048]{1,0:T(8,128)(2,1)}) %reduce-scatter.16.cloned.1.call-update) | async-done | bytes 524304
  670.7 154.3 %reduce-scatter.24.cloned.1.call-done = bf16[1,8,512,512]{3,2,1,0:T(8,128)(2,1)} async-done(((bf16[4,8,512,512]{3,2,1,0:T(8,128)(2,1)}), bf16[1,8,512,512]{3,2,1,0:T(8,128)(2,1)}) %reduce-scatter.24.cloned.1.call-update) | async-done | bytes 4194320
  825.0 170.5 %all-reduce.7 = (f32[1,8,512,512]{3,2,1,0:T(8,128)}, f32[1,2,512]{2,1,0:T(2,128)}) all-reduce(bf16[1,8,512,512]{3,2,1,0:T(8,128)(2,1)} %reduce-scatter.24.cloned.1.call-done, f32[1,2,512]{2,1,0:T(2,128)S(1)} %constant_dynamic-slice_fusion.5), channel_id=1, replica_groups=mesh['section'=4,'dp'=8] {'dp'}, use_global_device_ids=true, to_apply=%region_28.29 | all-reduce | flops 2098176 | bytes 12591104 | tf_op jit(solution)/shard_map/psum | solution.py:594
  (152 shorter events, 46.7 us)
Async XLA Ops:
  7.2 3.5 copy-start
  7.2 40.6 %all-gather.5.cloned.1.call-start = ((), (), s32[]{:S(2)}) async-start(), calls=%async_computation.5 | async-start | bytes 2621440 | tf_op jit(solution)/shard_map/all_gather | solution.py:570
  7.9 76.9 %all-gather.7.cloned.1.call-start = ((), (), s32[]{:S(2)}) async-start(), calls=%async_computation.6 | async-start | bytes 2621440 | tf_op jit(solution)/shard_map/all_gather | solution.py:570
  8.7 113.2 %all-gather.11.cloned.1.call-start = ((), (), s32[]{:S(2)}) async-start(), calls=%async_computation.8 | async-start | bytes 2621440 | tf_op jit(solution)/shard_map/all_gather | solution.py:570
  9.4 1.4 copy-start.11
  9.4 1.9 copy-start.12
  9.4 2.0 copy-start.13
  9.4 2.6 copy-start.8
  9.5 271.5 %all-gather.9.cloned.1.call-start = ((), (), s32[]{:S(2)}) async-start(), calls=%async_computation.7 | async-start | bytes 20971520 | tf_op jit(solution)/shard_map/all_gather | solution.py:580
  10.0 586.5 %reduce-scatter.18.cloned.1.call-start = ((), (), s32[]{:S(2)}) async-start(), calls=%async_computation.10 | async-start | bytes 327680
  10.1 11.7 %collective-permute-start.4 = (s32[8]{0:T(128)S(1)}, s32[8]{0:T(128)S(1)}, u32[]{:S(2)}, u32[]{:S(2)}) collective-permute-start(s32[8]{0:T(128)S(1)} %fusion.10), channel_id=1, source_target_pairs={{0,1},{1,0},{2,3},{3,2},{4,5},{5,4},{6,7},{7,6},{8,9},{9,8},{10,11... | collective-permute-start | bytes 104 | tf_op jit(solution)/shard_map/ppermute | solution.py:556
  10.7 14.1 %collective-permute-start.3 = (s32[1024]{0:T(1024)S(1)}, s32[1024]{0:T(1024)S(1)}, u32[]{:S(2)}, u32[]{:S(2)}) collective-permute-start(s32[1024]{0:T(1024)S(1)} %bitcast.146), channel_id=1, source_target_pairs={{0,1},{1,0},{2,3},{3,2},{4,5},{5,4},{6,7},{7,6},{8,9},{9,8},{10,11... | collective-permute-start | bytes 12296 | tf_op jit(solution)/shard_map/ppermute | solution.py:556
  10.8 19.2 %collective-permute-start.2 = (s32[1024]{0:T(1024)S(1)}, s32[1024]{0:T(1024)S(1)}, u32[]{:S(2)}, u32[]{:S(2)}) collective-permute-start(s32[1024]{0:T(1024)S(1)} %bitcast.140), channel_id=1, source_target_pairs={{0,1},{1,0},{2,3},{3,2},{4,5},{5,4},{6,7},{7,6},{8,9},{9,8},{10,11... | collective-permute-start | bytes 12296 | tf_op jit(solution)/shard_map/ppermute | solution.py:556
  11.3 12.8 %collective-permute-start.1 = (s32[1024]{0:T(1024)S(1)}, s32[1024]{0:T(1024)S(1)}, u32[]{:S(2)}, u32[]{:S(2)}) collective-permute-start(s32[1024]{0:T(1024)S(1)} %bitcast.148), channel_id=1, source_target_pairs={{0,1},{1,0},{2,3},{3,2},{4,5},{5,4},{6,7},{7,6},{8,9},{9,8},{10,11... | collective-permute-start | bytes 12296 | tf_op jit(solution)/shard_map/ppermute | solution.py:556
  11.5 10.4 %collective-permute-start = (s32[1024]{0:T(1024)S(1)}, s32[1024]{0:T(1024)S(1)}, u32[]{:S(2)}, u32[]{:S(2)}) collective-permute-start(s32[1024]{0:T(1024)S(1)} %bitcast.142), channel_id=1, source_target_pairs={{0,1},{1,0},{2,3},{3,2},{4,5},{5,4},{6,7},{7,6},{8,9},{9,8},{10,11... | collective-permute-start | bytes 12296 | tf_op jit(solution)/shard_map/ppermute | solution.py:556
  50.0 75.3 %collective-permute-start.5 = (bf16[1024,512]{1,0:T(8,128)(2,1)}, bf16[1024,512]{1,0:T(8,128)(2,1)}, u32[]{:S(2)}, u32[]{:S(2)}) collective-permute-start(bf16[1024,512]{1,0:T(8,128)(2,1)} %dynamic-slice_bitcast_fusion.2), channel_id=1, source_target_pairs={{0,1},{1,0},{2,3},{3,2},{4,5},{5,4},{6,7},{7,6},{8,9},{9,8},{10,11... | collective-permute-start | bytes 3145736 | tf_op jit(solution)/shard_map/ppermute | solution.py:556
  87.0 38.3 %copy-start.3 = (bf16[2,1024,512]{2,1,0:T(8,128)(2,1)S(1)}, bf16[2,1024,512]{2,1,0:T(8,128)(2,1)}, u32[]{:S(2)}) copy-start(bf16[2,1024,512]{2,1,0:T(8,128)(2,1)} %all-gather.5.cloned.1.call-done) | copy-start | bytes 6291460
  87.0 39.4 %collective-permute-start.6 = (bf16[1024,512]{1,0:T(8,128)(2,1)}, bf16[1024,512]{1,0:T(8,128)(2,1)}, u32[]{:S(2)}, u32[]{:S(2)}) collective-permute-start(bf16[1024,512]{1,0:T(8,128)(2,1)} %dynamic-slice_bitcast_fusion.1), channel_id=1, source_target_pairs={{0,1},{1,0},{2,3},{3,2},{4,5},{5,4},{6,7},{7,6},{8,9},{9,8},{10,11... | collective-permute-start | bytes 3145736 | tf_op jit(solution)/shard_map/ppermute | solution.py:556
  123.1 4.5 collective-permute-start.7
  124.5 2.0 copy-start.4
  126.5 2.0 copy-start.5
  443.2 89.9 %copy-start.2 = (f32[1024,512]{1,0:T(8,128)S(1)}, f32[1024,512]{1,0:T(8,128)}, u32[]{:S(2)}) copy-start(f32[1024,512]{1,0:T(8,128)} %get-tuple-element.83) | copy-start | bytes 6291460
  446.0 87.0 %collective-permute-start.11 = (bf16[1024,512]{1,0:T(8,128)(2,1)}, bf16[1024,512]{1,0:T(8,128)(2,1)}, u32[]{:S(2)}, u32[]{:S(2)}) collective-permute-start(bf16[1024,512]{1,0:T(8,128)(2,1)} %convert_element_type.135), channel_id=1, source_target_pairs={{0,1},{1,0},{2,3},{3,2},{4,5},{5,4},{6,7},{7,6},{8,9},{9,8},{10,11... | collective-permute-start | bytes 3145736 | tf_op jit(solution)/shard_map/ppermute | solution.py:556
  529.9 1.2 collective-permute-start.9
  532.7 65.5 %reduce-scatter.22.cloned.1.call-start = ((), (), s32[]{:S(2)}) async-start(), calls=%async_computation.12 | async-start | bytes 2621440
  542.6 1.6 copy-start.7
  542.6 87.0 %reduce-scatter.20.cloned.1.call-start = ((), (), s32[]{:S(2)}) async-start(), calls=%async_computation.11 | async-start | bytes 2621440
  544.3 2.7 collective-permute-start.10
  555.4 112.7 %reduce-scatter.16.cloned.1.call-start = ((), (), s32[]{:S(2)}) async-start(), calls=%async_computation.9 | async-start | bytes 2621440
  555.4 2.7 collective-permute-start.8
  566.4 258.6 %reduce-scatter.24.cloned.1.call-start = ((), (), s32[]{:S(2)}) async-start(), calls=%async_computation.13 | async-start | bytes 20971520
  669.5 326.0 %copy-start.1 = (s32[2,1024]{1,0:T(2,128)S(1)}, s32[2,1024]{1,0:T(2,128)}, u32[]{:S(2)}) copy-start(s32[2,1024]{1,0:T(2,128)} %param.18) | copy-start | bytes 24580
  (9 other events, 10.1 us)
Sparse Core Ops, SparseCore 0:
  9.8 37.8 all-gather.4
  49.6 35.1 all-gather.6
  86.6 35.1 all-gather.10
  123.5 157.4 all-gather.8
  532.8 20.0 reduce-scatter.17
  556.0 35.6 reduce-scatter.21
  594.6 34.9 reduce-scatter.19
  632.9 35.1 reduce-scatter.15
  671.1 153.8 reduce-scatter.23
